TPU v7x, 128 devices: a whole 4x4x4 slice. The times are simulated.
128 devices in a mesh: gx: 8 (over y, x_lo), gy: 16 (over z, x_hi, core).
Axes of the slice: x: 4 (x_hi: 2, x_lo: 2; x = x_hi * 2 + x_lo), y: 4, z: 4, core: 2. Of those that a mesh axis runs over, the one named last changes fastest.
Arguments:
- positions: float32 [8, 16, 3, 256], P('gx', 'gy'), may hold values from 0 to 1
- species: int32 [8, 16, 256], P('gx', 'gy'), may hold values from 0 to 88
- dest_key: int32 [8, 16, 256], P('gx', 'gy'), may hold values from 0 to 4, as said below
- send_list: int32 [8, 16, 4, 32], P('gx', 'gy'), may hold values from 0 to 255, as said below
- send_count: int32 [8, 16, 4], P('gx', 'gy'), may hold values from 8 to 32, as said below
- border: int32 [8, 16, 128], P('gx', 'gy'), may hold values from 0 to 255, as said below
- neighbours: int32 [8, 16, 384, 12], P('gx', 'gy'), may hold values from -1 to 1535, as said below
- embedding: float32 [89, 128], replicated, may hold values from -4 to 4
- radial_in: float32 [2, 8, 64], replicated, may hold values from -2 to 2
- radial_mid: float32 [2, 64, 64], replicated, may hold values from -0.75 to 0.75
- radial_out_one: float32 [64, 384], replicated, may hold values from -4 to 4
- radial_out_two: float32 [64, 896], replicated, may hold values from -4 to 4
- mix: float32 [2, 3, 128, 128], replicated, may hold values from -0.5 to 0.5
- mix_out_one: float32 [3, 128, 128], replicated, may hold values from -0.5 to 0.5
- mix_out_two: float32 [128, 128], replicated, may hold values from -0.5 to 0.5
- product_one: float32 [5, 128], replicated, may hold values from -4 to 4
- product_two: float32 [3, 128], replicated, may hold values from -4 to 4
- read_lin: float32 [128], replicated, may hold values from -0.5 to 0.5
- read_hidden: float32 [128, 16], replicated, may hold values from -0.5 to 0.5
- read_out: float32 [16], replicated, may hold values from -1.5 to 1.5
Outputs:
- atom_energy: float32 [8, 16, 384], P('gx', 'gy')
- forces: float32 [8, 16, 3, 384], P('gx', 'gy')
Inputs may be any that keep to these rules, and one draw needn't show every extreme that they name: `dest_key`: 0 keeps the atom; 1, 2, 3, 4 send it to the next device along gx, the previous along gx, the next along gy, the previous along gy (periodic); each device has at most 32 atoms of each nonzero key. `send_list`: row d holds in increasing order the slots whose dest_key is d + 1, then other slots as padding. `send_count`: the number of slots whose dest_key is d + 1; some device has exactly 32 in some direction in every draw. `border`: distinct slots whose dest_key is 0. `neighbours`: -1 marks an empty slot; a value below 384 is a local row after migration; 384 + (3 * a + b) * 128 + k is the k-th border row of the device at offset (a - 1, b - 1) along (gx, gy), with (a, b) never (1, 1); devices differ in how many slots are empty.
All inputs are finite; a program needn't handle non-finite values.
Results may differ from a plain program's by a relative error of at most 0.003.
Values may be sent and summed in bfloat16 or wider, within the bound.
No kernel may reach another device: no remote copies, remote signals or barrier semaphores. Data moves between devices by JAX's collectives and lax.ppermute only.
A program may use at most 192 MiB of HBM per device.

v0:
```python
import math

import jax
import jax.numpy as jnp
from jax import lax
from jax.sharding import PartitionSpec as P

cutoff_radius = 5.0
cell_side = 1.0
highest = lax.Precision.HIGHEST


def from_behind(block, axis, distance):
    devices = range(lax.axis_size(axis))
    route = [((i - distance) % len(devices), i) for i in devices]
    return lax.ppermute(block, axis, route)


def as_sent(array):

    def short(part):
        return part.astype(jnp.bfloat16) if part.dtype == jnp.float32 else part

    return jax.tree.map(short, array)


def extended(array, sides, width):
    for axis, dim in sides:
        count, length = (lax.axis_size(axis), array.shape[dim])
        up = [(i, (i + 1) % count) for i in range(count)]
        down = [(j, i) for i, j in up]
        last = lax.slice_in_dim(array, length - width, length, axis=dim)
        first = lax.slice_in_dim(array, 0, width, axis=dim)
        before = lax.ppermute(last, axis, up)
        after = lax.ppermute(first, axis, down)
        array = jnp.concatenate([before, array, after], axis=dim)
    return array


def geometry(offsets, basis_count):
    squared = jnp.sum(offsets * offsets, axis=0) + 1.0
    distance = jnp.sqrt(squared)
    pointer = offsets / distance[None, :]
    scaled = distance / cutoff_radius
    sixth = scaled * scaled * scaled * scaled * scaled * scaled
    envelope = 1.0 - 28.0 * sixth + 48.0 * sixth * scaled - 21.0 * sixth * scaled * scaled
    orders = jnp.arange(1, basis_count + 1).astype(jnp.float32)[:, None]
    basis = (
        math.sqrt(2.0 / cutoff_radius)
        * jnp.sin(orders * (math.pi / cutoff_radius) * distance[None, :])
        * (envelope / distance)[None, :]
    )
    along_x = pointer[0]
    along_y = pointer[1]
    along_z = pointer[2]
    root_five = math.sqrt(5.0)
    root_fifteen = math.sqrt(15.0)
    vector_part = math.sqrt(3.0) * pointer
    tensor_part = jnp.stack(
        [
            root_fifteen * along_x * along_y,
            root_fifteen * along_y * along_z,
            0.5 * root_five * (2.0 * along_z * along_z - along_x * along_x - along_y * along_y),
            root_fifteen * along_x * along_z,
            0.5 * root_fifteen * (along_x * along_x - along_y * along_y),
        ]
    )
    return (basis, vector_part, tensor_part)


def radial(basis, w_in, w_mid, w_out):
    hidden = jax.nn.silu(jnp.dot(w_in.T, basis, precision=highest))
    hidden = jax.nn.silu(jnp.dot(w_mid.T, hidden, precision=highest))
    return jnp.dot(w_out.T, hidden, precision=highest)


def contract(matrix, values):
    return jnp.einsum("cd,...cn->...dn", matrix, values, precision=highest)


def interaction(
    first, pos_all, feats_all, occ_all, neighbour_block, pos_block, occ_block, residual, weights
):
    w_in, w_mid, w_out, mixing, mixing_out, coefs = weights
    atoms, slots = neighbour_block.shape
    channels = mixing.shape[-1]
    flat_index = jnp.maximum(neighbour_block, 0).reshape(-1)
    edge_mask = (
        (neighbour_block >= 0).astype(jnp.float32).reshape(-1)
        * occ_all[flat_index]
        * jnp.repeat(occ_block, slots)
    )
    offsets = pos_all[:, flat_index] - jnp.repeat(pos_block, slots, axis=1)
    basis, vector_part, tensor_part = geometry(offsets, w_in.shape[0])
    source = feats_all[:, flat_index] * edge_mask[None, :]
    paths = 3 if first else 7
    edge_weights = radial(basis, w_in, w_mid, w_out).reshape(paths, channels, -1)
    scalar = source[:channels]
    if first:
        msg_scalar = edge_weights[0] * scalar
        msg_vector = edge_weights[1][None] * scalar[None] * vector_part[:, None]
        msg_tensor = edge_weights[2][None] * scalar[None] * tensor_part[:, None]
    else:
        vectors = source[channels : 4 * channels].reshape(3, channels, -1)
        tensors = source[4 * channels :].reshape(5, channels, -1)
        msg_scalar = (
            edge_weights[0] * scalar
            + edge_weights[1] * jnp.sum(vector_part[:, None] * vectors, axis=0)
            + edge_weights[2] * jnp.sum(tensor_part[:, None] * tensors, axis=0)
        )
        msg_vector = (
            edge_weights[3][None] * scalar[None] * vector_part[:, None]
            + edge_weights[4][None] * vectors
        )
        msg_tensor = (
            edge_weights[5][None] * scalar[None] * tensor_part[:, None]
            + edge_weights[6][None] * tensors
        )

    def pooling(message):
        return jnp.sum(message.reshape(message.shape[:-1] + (atoms, slots)), axis=-1) / slots

    mixed_scalar = contract(mixing[0], pooling(msg_scalar))
    mixed_vector = contract(mixing[1], pooling(msg_vector))
    mixed_tensor = contract(mixing[2], pooling(msg_tensor))
    product_scalar = (
        mixed_scalar
        + coefs[0][:, None] * mixed_scalar * mixed_scalar
        + coefs[1][:, None] * jnp.sum(mixed_vector * mixed_vector, axis=0)
        + coefs[2][:, None] * jnp.sum(mixed_tensor * mixed_tensor, axis=0)
    )
    if first:
        product_vector = mixed_vector * (1.0 + coefs[3][:, None] * mixed_scalar)[None]
        product_tensor = mixed_tensor * (1.0 + coefs[4][:, None] * mixed_scalar)[None]
        new_scalar = contract(mixing_out[0], product_scalar) + residual
        new_vector = contract(mixing_out[1], product_vector).reshape(3 * channels, atoms)
        new_tensor = contract(mixing_out[2], product_tensor).reshape(5 * channels, atoms)
        return jnp.concatenate([new_scalar, new_vector, new_tensor], axis=0)
    return contract(mixing_out, product_scalar) + residual[:channels]


def run_layer(first, pos_all, feats_all, occ_all, occupied, neighbour_rows, weights):
    total_rows = neighbour_rows.shape[0]
    block_rows = math.gcd(total_rows, 128)
    block_count = total_rows // block_rows

    def one_block(block_index):
        start = block_index * block_rows
        neighbour_block = lax.dynamic_slice_in_dim(neighbour_rows, start, block_rows, 0)
        pos_block = lax.dynamic_slice_in_dim(pos_all, start, block_rows, 1)
        occ_block = lax.dynamic_slice_in_dim(occupied, start, block_rows, 0)
        residual = lax.dynamic_slice_in_dim(feats_all, start, block_rows, 1)
        return interaction(
            first,
            pos_all,
            feats_all,
            occ_all,
            neighbour_block,
            pos_block,
            occ_block,
            residual,
            weights,
        )

    outputs = lax.map(jax.checkpoint(one_block), jnp.arange(block_count, dtype=jnp.int32))
    return jnp.moveaxis(outputs, 0, 1).reshape(outputs.shape[1], total_rows)


def shift_table():
    grid_shift = cell_side * (jnp.arange(3).astype(jnp.float32) - 1.0)
    first_axis = jnp.broadcast_to(grid_shift[:, None], (3, 3))
    second_axis = jnp.broadcast_to(grid_shift[None, :], (3, 3))
    return jnp.stack([first_axis, second_axis, jnp.zeros((3, 3), jnp.float32)], axis=-1)


def give_back_features(pieces):
    column = pieces[:, 1]
    for alongside, stride in ((0, -1), (2, 1)):
        column = column + from_behind(
            pieces[:, alongside].astype(jnp.bfloat16), "gy", stride
        ).astype(jnp.float32)
    total = column[1]
    for across, stride in ((0, -1), (2, 1)):
        total = total + from_behind(as_sent(column[across]), "gx", stride)
    return total


def give_back_coords(pieces):
    column = pieces[:, 1]
    for alongside, stride in ((0, -1), (2, 1)):
        column = column + from_behind(pieces[:, alongside], "gy", stride)
    total = column[1]
    for across, stride in ((0, -1), (2, 1)):
        total = total + from_behind(column[across], "gx", stride)
    return total


def on_device(
    positions,
    species,
    dest_key,
    send_list,
    send_count,
    border,
    neighbours,
    embedding,
    radial_in,
    radial_mid,
    radial_out_one,
    radial_out_two,
    mix,
    mix_out_one,
    mix_out_two,
    product_one,
    product_two,
    read_lin,
    read_hidden,
    read_out,
):
    own_coords = positions[0, 0]
    own_kinds = species[0, 0]
    staying = (dest_key[0, 0] == 0).astype(jnp.float32)
    listed = send_list[0, 0]
    counted = send_count[0, 0]
    edge_lists = neighbours[0, 0]
    border_rows = border[0, 0]
    slot_count = listed.shape[1]
    border_count = border_rows.shape[0]
    channels = embedding.shape[1]
    slot_used = jnp.arange(slot_count)[None, :] < counted[:, None]
    leaving_kinds = jnp.where(slot_used, own_kinds[listed], -1).astype(jnp.float32)
    leaving = jnp.concatenate(
        [jnp.moveaxis(jnp.take(own_coords, listed, axis=1), 1, 0), leaving_kinds[:, None, :]],
        axis=1,
    )
    border_packet = jnp.concatenate(
        [own_coords[:, border_rows], own_kinds[border_rows].astype(jnp.float32)[None, :]], axis=0
    )
    arrived = [leaving[0], leaving[1], leaving[2], leaving[3]]
    for target, stride in ((0, 1), (1, -1)):
        arrived[target] = from_behind(leaving[target], "gx", stride)
    for target, stride in ((2, 1), (3, -1)):
        arrived[target] = from_behind(leaving[target], "gy", stride)
    beside_all = extended(border_packet[None, None], (("gx", 0), ("gy", 1)), 1)
    arrival_moves = ((0, -1.0), (0, 1.0), (1, -1.0), (1, 1.0))
    adjusted = []
    for target in range(4):
        coordinate, amount = arrival_moves[target]
        adjusted.append(arrived[target].at[coordinate].add(amount * cell_side))
    incoming = jnp.concatenate(adjusted, axis=1)
    local_coords = jnp.concatenate([own_coords, incoming[:3]], axis=1)
    local_kinds = jnp.concatenate([own_kinds, incoming[3].astype(jnp.int32)])
    occupied = jnp.concatenate([staying, (incoming[3] >= 0).astype(jnp.float32)])
    ghost_block = beside_all[:, :, :3, :] + shift_table()[:, :, :, None]
    ghost_coords = jnp.moveaxis(ghost_block, 2, 0).reshape(3, 9 * border_count)
    ghost_kinds = beside_all[:, :, 3, :].reshape(9 * border_count).astype(jnp.int32)
    coords_all = jnp.concatenate([local_coords, ghost_coords], axis=1)
    kinds_all = jnp.maximum(jnp.concatenate([local_kinds, ghost_kinds]), 0)
    occupied_all = jnp.concatenate([occupied, jnp.ones((9 * border_count,), jnp.float32)])
    one_hot = (kinds_all[None, :] == jnp.arange(embedding.shape[0])[:, None]).astype(jnp.float32)
    initial = jnp.dot(embedding.T, one_hot, precision=highest)
    first_weights = (radial_in[0], radial_mid[0], radial_out_one, mix[0], mix_out_one, product_one)
    second_weights = (radial_in[1], radial_mid[1], radial_out_two, mix[1], mix_out_two, product_two)

    def first_layer(coords_in):
        return run_layer(
            True, coords_in, initial, occupied_all, occupied, edge_lists, first_weights
        )

    hidden_one, pull_one = jax.vjp(first_layer, coords_all)
    rounded = hidden_one.astype(jnp.bfloat16)
    border_feats = rounded[:, border_rows]
    partial_feats = extended(border_feats[None, None], (("gx", 0),), 1)
    around_feats = extended(partial_feats, (("gy", 1),), 1)
    ghost_feats = jnp.moveaxis(around_feats, 2, 0).reshape(rounded.shape[0], 9 * border_count)
    table = jnp.concatenate([rounded, ghost_feats], axis=1).astype(jnp.float32)

    def second_layer(coords_in, table_in):
        scalars = run_layer(
            False, coords_in, table_in, occupied_all, occupied, edge_lists, second_weights
        )
        readout = jax.nn.silu(jnp.dot(read_hidden.T, scalars, precision=highest))
        return occupied * jnp.dot(read_out, readout, precision=highest)

    energy_two, pull_two = jax.vjp(second_layer, coords_all, table)
    energy_one = occupied * jnp.dot(
        read_lin, rounded[:channels].astype(jnp.float32), precision=highest
    )
    atom_energy = energy_one + energy_two
    coords_grad_two, table_grad = pull_two(jnp.ones_like(energy_two))
    local_rows = occupied.shape[0]
    feats_grad = table_grad[:, :local_rows].at[:channels].add(read_lin[:, None] * occupied[None, :])
    ghost_grad = jnp.moveaxis(
        table_grad[:, local_rows:].reshape(table_grad.shape[0], 3, 3, border_count), 0, 2
    )
    feats_grad = feats_grad.at[:, border_rows].add(give_back_features(ghost_grad))
    (coords_grad_one,) = pull_one(feats_grad)
    coords_grad = coords_grad_one + coords_grad_two
    ghost_coords_grad = jnp.moveaxis(
        coords_grad[:, local_rows:].reshape(3, 3, 3, border_count), 0, 2
    )
    forces = (
        -coords_grad[:, :local_rows].at[:, border_rows].add(give_back_coords(ghost_coords_grad))
    )
    return (atom_energy[None, None], forces[None, None])


def solution(mesh):
    in_specs = (
        P("gx", "gy", None, None),
        P("gx", "gy", None),
        P("gx", "gy", None),
        P("gx", "gy", None, None),
        P("gx", "gy", None),
        P("gx", "gy", None),
        P("gx", "gy", None, None),
        P(),
        P(),
        P(),
        P(),
        P(),
        P(),
        P(),
        P(),
        P(),
        P(),
        P(),
        P(),
        P(),
    )
    out_specs = (P("gx", "gy", None), P("gx", "gy", None, None))
    return jax.shard_map(
        on_device, mesh=mesh, in_specs=in_specs, out_specs=out_specs, check_vma=False
    )
```

profile of v0, /device:TPU:26, one launch (start us, length us, event | category | flops | bytes accessed | tf_op | source)
XLA Modules:
  0.0 1781.3 jit_solution(15009213149578226570)
XLA Ops:
  50.7 132.6 %while.59 = (s32[]{:T(128)}, bf16[3,1152,128]{1,2,0:T(8,128)(2,1)}, s32[3]{0:T(128)S(1)}, s32[384,12]{1,0:T(8,128)S(1)}, f32[3,1536]{0,1:T(8,128)}, /*index=5*/f...) while((s32[]{:T(128)}, bf16[3,1152,128]{1,2,0:T(8,128)(2,1)}, ...), condition=%wide.region_7.8_spmd.clone, body=%wide.region_0.7_spmd.clone.sunk | while | flops 997599232 | bytes 40897072 | solution.py:165
  201.3 15.5 collective-permute-done.11
  221.7 346.2 %while.60 = (s32[]{:T(128)}, f32[3,128,128]{1,2,0:T(8,128)}, s32[3]{0:T(128)S(1)}, s32[384,12]{1,0:T(8,128)S(1)}, f32[3,1536]{0,1:T(8,128)}, /*index=5*/f32[64,8...) while((s32[]{:T(128)}, f32[3,128,128]{1,2,0:T(8,128)}, ...), condition=%wide.region_17.18_spmd.clone, body=%wide.region_8.17_spmd.clone.sunk | while | flops 1407217152 | bytes 156353264 | solution.py:165
  223.6 11.4 gather_fusion.3
  338.9 11.4 gather_fusion.3
  454.1 11.4 gather_fusion.3
  570.5 824.9 %while.61 = (s32[]{:T(128)}, f32[3,1536]{0,1:T(8,128)}, f32[1152,1536]{0,1:T(8,128)}, s32[3]{0:T(128)S(1)}, f32[3,128,128]{1,2,0:T(8,128)S(1)}, /*index=5*/s32[3...) while((s32[]{:T(128)}, f32[3,1536]{0,1:T(8,128)}, ...), condition=%wide.region_39.40_spmd.clone, body=%wide.region_18.39_spmd.clone.sunk | while | flops 2815792640 | bytes 465380640 | solution.py:165
  579.0 11.5 gather_fusion.7
  671.3 9.5 multiply_reduce_fusion.68
  726.6 9.3 multiply_reduce_fusion.69
  772.6 9.1 scatter_custom_fusion.21
  815.3 18.8 %scatter_custom_fusion.22 = f32[1152,1536]{0,1:T(8,128)} fusion(s32[1536]{0:T(1024)} %copy-done.105, f32[1536,1152]{1,0:T(8,128)} %copy.863, f32[]{:T(128)} %constant.686.clone.1..sunk.1), kind=kCustom, calls=%fused_computation.223.clone.1 | custom fusion | flops 1769472 | bytes 7078400 | tf_op jit(solution)/shard_map/transpose(jvp())/while/body/eval_jaxpr/checkpoint/scatter-add | solution.py:95
  851.2 11.5 gather_fusion.7
  943.7 9.5 multiply_reduce_fusion.68
  1044.8 9.1 scatter_custom_fusion.21
  1087.5 18.8 %scatter_custom_fusion.22 = f32[1152,1536]{0,1:T(8,128)} fusion(s32[1536]{0:T(1024)} %copy-done.105, f32[1536,1152]{1,0:T(8,128)} %copy.863, f32[]{:T(128)} %constant.686.clone.1..sunk.1), kind=kCustom, calls=%fused_computation.223.clone.1 | custom fusion | flops 1769472 | bytes 7078400 | tf_op jit(solution)/shard_map/transpose(jvp())/while/body/eval_jaxpr/checkpoint/scatter-add | solution.py:95
  1125.6 11.5 gather_fusion.7
  1217.9 9.5 multiply_reduce_fusion.68
  1273.2 9.1 multiply_reduce_fusion.69
  1319.0 9.1 scatter_custom_fusion.21
  1361.9 18.8 %scatter_custom_fusion.22 = f32[1152,1536]{0,1:T(8,128)} fusion(s32[1536]{0:T(1024)} %copy-done.105, f32[1536,1152]{1,0:T(8,128)} %copy.863, f32[]{:T(128)} %constant.686.clone.1..sunk.1), kind=kCustom, calls=%fused_computation.223.clone.1 | custom fusion | flops 1769472 | bytes 7078400 | tf_op jit(solution)/shard_map/transpose(jvp())/while/body/eval_jaxpr/checkpoint/scatter-add | solution.py:95
  1410.3 15.7 collective-permute-done.13
  1452.8 304.1 %while.62 = (s32[]{:T(128)}, f32[3,1536]{0,1:T(8,128)}, s32[3]{0:T(128)}, f32[3,1152,128]{2,1,0:T(8,128)}, s32[384,12]{1,0:T(8,128)S(1)}, /*index=5*/f32[3,1536]...) while((s32[]{:T(128)}, f32[3,1536]{0,1:T(8,128)}, ...), condition=%wide.region_57.58_spmd.clone, body=%wide.region_41.57_spmd.clone.sunk | while | flops 1771674112 | bytes 99862632 | solution.py:165
  1745.2 9.1 scatter_custom_fusion.24
  (2040 shorter events, 1503.7 us)
Async XLA Ops:
  5.7 30.6 %collective-permute-start.5 = (f32[1,1,4,128]{3,2,1,0:T(4,128)S(1)}, f32[1,1,4,128]{3,2,1,0:T(4,128)S(1)}, u32[]{:S(2)}, u32[]{:S(2)}) collective-permute-start(f32[1,1,4,128]{3,2,1,0:T(4,128)S(1)} %maximum_bitcast_fusion.1), channel_id=1, source_target_pairs={{16,0},{32,16},{48,32},{64,48},{80,64},{96,80},{112,96},{0,112},{1... | collective-permute-start | bytes 6152 | tf_op jit(solution)/shard_map/ppermute | solution.py:35
  6.3 30.0 %collective-permute-start.4 = (f32[1,1,4,128]{3,2,1,0:T(4,128)S(1)}, f32[1,1,4,128]{3,2,1,0:T(4,128)S(1)}, u32[]{:S(2)}, u32[]{:S(2)}) collective-permute-start(f32[1,1,4,128]{3,2,1,0:T(4,128)S(1)} %maximum_bitcast_fusion.1), channel_id=1, source_target_pairs={{0,16},{16,32},{32,48},{48,64},{64,80},{80,96},{96,112},{112,0},{1... | collective-permute-start | bytes 6152 | tf_op jit(solution)/shard_map/ppermute | solution.py:34
  14.6 16.1 collective-permute-start.3
  19.1 15.7 collective-permute-start.2
  19.1 15.7 collective-permute-start.1
  30.7 5.4 collective-permute-start
  36.4 5.6 collective-permute-start.7
  40.7 6.7 collective-permute-start.6
  185.9 9.6 collective-permute-start.9
  186.4 9.2 collective-permute-start.8
  196.6 20.2 %collective-permute-start.11 = (bf16[3,1,1152,128]{2,3,1,0:T(8,128)(2,1)}, bf16[3,1,1152,128]{2,3,1,0:T(8,128)(2,1)}, u32[]{:S(2)}, u32[]{:S(2)}) collective-permute-start(bf16[3,1,1152,128]{2,3,1,0:T(8,128)(2,1)} %pad_maximum_fusion.1), channel_id=1, source_target_pairs={{1,0},{2,1},{3,2},{4,3},{5,4},{6,5},{7,6},{8,7},{9,8},{10,9},{11,1... | collective-permute-start | bytes 2654216 | tf_op jit(solution)/shard_map/ppermute | solution.py:35
  198.3 18.6 %collective-permute-start.10 = (bf16[3,1,1152,128]{2,3,1,0:T(8,128)(2,1)}, bf16[3,1,1152,128]{2,3,1,0:T(8,128)(2,1)}, u32[]{:S(2)}, u32[]{:S(2)}) collective-permute-start(bf16[3,1,1152,128]{2,3,1,0:T(8,128)(2,1)} %pad_maximum_fusion.1), channel_id=1, source_target_pairs={{0,1},{1,2},{2,3},{3,4},{4,5},{5,6},{6,7},{7,8},{8,9},{9,10},{10,1... | collective-permute-start | bytes 2654216 | tf_op jit(solution)/shard_map/ppermute | solution.py:34
  221.7 346.2 %copy-start.124 = (f32[128,16]{0,1:T(8,128)S(1)}, f32[128,16]{0,1:T(8,128)}, u32[]{:S(2)}) copy-start(f32[128,16]{0,1:T(8,128)} %param.56) | copy-start | bytes 24580
  579.0 57.8 %copy-start.76 = (f32[1536]{0:T(1024)}, f32[1536]{0:T(1024)S(1)}, u32[]{:S(2)}) copy-start(f32[1536]{0:T(1024)S(1)} %get-tuple-element.2376) | copy-start | bytes 18436 | tf_op jit(solution)/shard_map/transpose(jvp())/while
  851.2 57.8 %copy-start.76 = (f32[1536]{0:T(1024)}, f32[1536]{0:T(1024)S(1)}, u32[]{:S(2)}) copy-start(f32[1536]{0:T(1024)S(1)} %get-tuple-element.2376) | copy-start | bytes 18436 | tf_op jit(solution)/shard_map/transpose(jvp())/while
  1125.6 57.8 %copy-start.76 = (f32[1536]{0:T(1024)}, f32[1536]{0:T(1024)S(1)}, u32[]{:S(2)}) copy-start(f32[1536]{0:T(1024)S(1)} %get-tuple-element.2376) | copy-start | bytes 18436 | tf_op jit(solution)/shard_map/transpose(jvp())/while
  1400.8 25.2 %collective-permute-start.13 = (bf16[3,1152,128]{1,2,0:T(8,128)(2,1)S(1)}, bf16[3,1152,128]{1,2,0:T(8,128)(2,1)S(1)}, u32[]{:S(2)}, u32[]{:S(2)}) collective-permute-start(bf16[3,1152,128]{1,2,0:T(8,128)(2,1)S(1)} %get-tuple-element.1719), channel_id=1, source_target_pairs={{15,0},{0,1},{1,2},{2,3},{3,4},{4,5},{5,6},{6,7},{7,8},{8,9},{9,10... | collective-permute-start | bytes 2654216 | tf_op jit(solution)/shard_map/ppermute | solution.py:16
  1400.9 25.1 %collective-permute-start.12 = (bf16[3,1152,128]{1,2,0:T(8,128)(2,1)S(1)}, bf16[3,1152,128]{1,2,0:T(8,128)(2,1)}, u32[]{:S(2)}, u32[]{:S(2)}) collective-permute-start(bf16[3,1152,128]{1,2,0:T(8,128)(2,1)S(1)} %get-tuple-element.1718), channel_id=1, source_target_pairs={{1,0},{2,1},{3,2},{4,3},{5,4},{6,5},{7,6},{8,7},{9,8},{10,9},{11,1... | collective-permute-start | bytes 2654216 | tf_op jit(solution)/shard_map/ppermute | solution.py:16
  1428.8 12.9 collective-permute-start.15
  1434.2 12.4 collective-permute-start.14
  1758.5 10.4 collective-permute-start.17
  1758.6 10.3 collective-permute-start.16
  1769.0 5.4 collective-permute-start.19
  1772.5 6.4 collective-permute-start.18
  (412 other events, 2786.0 us)
where the time goes:
time: 1800 us; the launch traced here: 1780 us
  local copies, waits for them, and re-layouts  894 us (50%)
  other arithmetic  530 us (29%)
  matrix products  213 us (12%)
  waiting for transfers between devices  62.7 us (3%)
  starting transfers between devices  43.8 us (2%)
  loops' own time  36.6 us (2%)
    gather x24, local copies, waits for them, and re-layouts, interaction(): source = feats_all[:, flat_index] * edge_mask[None, :]  125 us
    gather x18, local copies, waits for them, and re-layouts, interaction(): occ_all[flat_index]  101 us
    dot_general x78, matrix products, contract(): return jnp.einsum('cd,...cn->...dn', matrix, values, precision=highest)  98.4 us
    reduce_sum x36, other arithmetic, pooling(): jnp.sum(message.reshape(message.shape[:-1] + (atoms, slots)), axis=-1)  86.6 us
    dot_general x18, matrix products, radial(): return jnp.dot(w_out.T, hidden, precision=highest)  75 us
    gather x39, local copies, waits for them, and re-layouts, interaction(): offsets = pos_all[:, flat_index] - jnp.repeat(pos_block, slots, axis=1)  56.9 us
    scatter-add x3, other arithmetic, interaction(): source = feats_all[:, flat_index] * edge_mask[None, :]  56.5 us
    scatter-add x6, other arithmetic, interaction(): offsets = pos_all[:, flat_index] - jnp.repeat(pos_block, slots, axis=1)  54.4 us
  transfers between devices with their start and end apart: 20, of which 11 were waited for; matrix products, arithmetic and copies ran while one was open for 2% of the time, Pallas kernels for 0%

commit v1 on v0

v1 whole, which is shorter than its diff:
```python
import functools
import math

import jax
import jax.numpy as jnp
from jax import lax
from jax.experimental import pallas as pl
from jax.experimental.pallas import tpu as pltpu
from jax.sharding import PartitionSpec as P

f32 = jnp.float32
bf16 = jnp.bfloat16
CH = 128
HID = 64
SLOTS = 12
LANES = 128
EDGES = SLOTS * LANES
LOCAL = 3
COLS = 11 * LANES
RADIUS = 5.0
SCALE = math.sqrt(2.0 / RADIUS)
R3 = math.sqrt(3.0)
R5 = math.sqrt(5.0)
R15 = math.sqrt(15.0)
VMEM = pl.BlockSpec(memory_space=pltpu.VMEM)
SMEM = pl.BlockSpec(memory_space=pltpu.SMEM)
LIMIT = 60 * 1024 * 1024


def call(kernel, out_shape, scratch=(), flops=1000000, in_specs=None, **kw):
    return pl.pallas_call(
        kernel,
        out_shape=out_shape,
        scratch_shapes=list(scratch),
        compiler_params=pltpu.CompilerParams(vmem_limit_bytes=LIMIT),
        cost_estimate=pl.CostEstimate(flops=flops, bytes_accessed=1000000, transcendentals=0),
        **({"in_specs": in_specs} if in_specs is not None else {}),
        **kw,
    )


def shape(*dims, kind=f32):
    return jax.ShapeDtypeStruct(dims, kind)


def lanes(i, n=1):
    return slice(i * LANES, (i + n) * LANES)


def hi_lo(x):
    hi = x.astype(bf16)
    return hi, (x - hi.astype(f32)).astype(bf16)


def split3(x):
    hi, lo = hi_lo(x)
    return jnp.concatenate([hi, lo, hi], axis=0)


def mm(a, b):
    return jnp.dot(a, b, preferred_element_type=f32)


def mm_nt(a, b):
    return lax.dot_general(a, b, (((1,), (1,)), ((), ())), preferred_element_type=f32)


def silu_parts(x):
    s = 0.5 * jnp.tanh(0.5 * x) + 0.5
    h = x * s
    return h, s + h * (1.0 - s)


def take_lanes(chunk, index):
    return jnp.take_along_axis(chunk, index, axis=1, mode="promise_in_bounds")


def gather_columns(ref, rows, index, chunks):
    low = index & 127
    block = index >> 7
    out = take_lanes(ref[rows, lanes(0)], low)
    for c in range(1, chunks):
        out = jnp.where(block == c, take_lanes(ref[rows, lanes(c)], low), out)
    return out


def packet_kernel(pos, spec, listed, border, count, out, tbl):
    tbl[...] = jnp.zeros_like(tbl)
    tbl[0:3, :] = pos[...]
    tbl[3:4, :] = spec[...].astype(f32)
    row = lax.broadcasted_iota(jnp.int32, (8, LANES), 0)
    lane = lax.broadcasted_iota(jnp.int32, (8, LANES), 1)
    way = lane >> 5
    index = jnp.broadcast_to(listed[...], (8, LANES))
    got = gather_columns(tbl, slice(0, 8), index, 2)
    amount = jnp.where(way == 0, count[0], jnp.where(way == 1, count[1], jnp.where(way == 2, count[2], count[3])))
    step = jnp.where((way & 1) == 0, -1.0, 1.0).astype(f32)
    got = got + jnp.where(row == (way >> 1), step, 0.0)
    got = jnp.where((row == 3) & ((lane & 31) >= amount), -1.0, got)
    out[:, lanes(0)] = got
    out[:, lanes(1)] = gather_columns(tbl, slice(0, 8), jnp.broadcast_to(border[...], (8, LANES)), 2)


PLACE = {1: 3, 7: 4, 0: 5, 3: 6, 6: 7, 2: 8, 5: 9, 8: 10}


def edges_kernel(pos, spec, key, xp, xn, yp, yn, nbr, border, geo, bgeo, vcol, kinds, occ, tbl):
    tbl[...] = jnp.zeros_like(tbl)
    tbl[0:3, 0:256] = pos[...]
    tbl[3:4, 0:256] = spec[...].astype(f32)
    tbl[4:5, 0:256] = (key[...] == 0).astype(f32)
    row = lax.broadcasted_iota(jnp.int32, (8, LANES), 0)
    way = lax.broadcasted_iota(jnp.int32, (8, LANES), 1) >> 5
    came = jnp.where(
        way == 0,
        xp[:, lanes(0)],
        jnp.where(way == 1, xn[:, lanes(0)], jnp.where(way == 2, yp[:, lanes(0)], yn[:, lanes(0)])),
    )
    tbl[:, lanes(2)] = came
    tbl[4:5, lanes(2)] = (came[3:4] >= 0).astype(f32)

    def ghost(place, block, dx, dy):
        moved = block + jnp.where(row == 0, dx, jnp.where(row == 1, dy, jnp.where(row == 4, 1.0, 0.0)))
        tbl[:, lanes(place)] = moved

    ghost(3, xp[:, lanes(1)], -1.0, 0.0)
    ghost(4, xn[:, lanes(1)], 1.0, 0.0)
    for base, got, dy in ((5, yp, -1.0), (8, yn, 1.0)):
        ghost(base, got[:, lanes(2)], -1.0, dy)
        ghost(base + 1, got[:, lanes(1)], 0.0, dy)
        ghost(base + 2, got[:, lanes(3)], 1.0, dy)
    kinds[...] = jnp.maximum(tbl[3:4, :], 0.0)
    occ[...] = tbl[4:5, 0 : LOCAL * LANES]
    geo[...] = jnp.zeros_like(geo)
    vcol[...] = jnp.full_like(vcol, -1)
    for b in range(LOCAL):
        own = tbl[:, lanes(b)]
        for s in range(SLOTS):
            n = nbr[s : s + 1, lanes(b)]
            old = n >> 7
            block = jnp.minimum(old, 2)
            for was, now in PLACE.items():
                block = jnp.where(old == was + 3, now, block)
            col = jnp.maximum(block, 0) * 128 + (n & 127)
            got = gather_columns(tbl, slice(0, 8), jnp.broadcast_to(col, (8, LANES)), 11)
            valid = (n >= 0) & (got[4:5] > 0.5) & (own[4:5] > 0.5)
            off = got - own
            val = jnp.where(row < 3, off, jnp.where(jnp.broadcast_to(valid, (8, LANES)), got, -1.0))
            geo[b, pl.ds(s, 4, stride=16), :] = val[0:4]
            vcol[b, s : s + 1, :] = jnp.where(valid, col, -1)
    index = jnp.broadcast_to(border[...], (8, LANES))
    low = index & 127
    for t in range(8):
        rows = slice(t * 8, t * 8 + 8)
        bgeo[rows, :] = jnp.where(
            (index >> 7) == 0, take_lanes(geo[0, rows, :], low), take_lanes(geo[1, rows, :], low)
        )


def geometry(ox, oy, oz):
    d = jnp.sqrt(ox * ox + oy * oy + oz * oz + 1.0)
    rd = 1.0 / d
    u = (ox * rd, oy * rd, oz * rd)
    t = d * (1.0 / RADIUS)
    t2 = t * t
    t5 = t2 * t2 * t
    t6 = t5 * t
    env = 1.0 - 28.0 * t6 + 48.0 * t6 * t - 21.0 * t6 * t2
    theta = (math.pi / RADIUS) * d
    s1, c1 = jnp.sin(theta), jnp.cos(theta)
    sines, cosines = [s1], [c1]
    before_s, before_c = jnp.zeros_like(s1), jnp.ones_like(c1)
    for _ in range(7):
        ns = 2.0 * c1 * sines[-1] - before_s
        nc = 2.0 * c1 * cosines[-1] - before_c
        before_s, before_c = sines[-1], cosines[-1]
        sines.append(ns)
        cosines.append(nc)
    slope = (-168.0 * t5 + 336.0 * t6 - 168.0 * t6 * t) * (1.0 / RADIUS)
    return u, d, rd, env, slope, sines, cosines


def harmonics(u):
    x, y, z = u
    return [
        R3 * x,
        R3 * y,
        R3 * z,
        R15 * x * y,
        R15 * y * z,
        0.5 * R5 * (2.0 * z * z - x * x - y * y),
        R15 * x * z,
        0.5 * R15 * (x * x - y * y),
    ]


def place_geometry(geo, yref, basrow, bas):
    u, d, rd, env, slope, sines, cosines = geo
    for k, h in enumerate(harmonics(u)):
        yref[k * 16 : k * 16 + 16, :] = h
    factor = SCALE * env * rd
    for m in range(8):
        basrow[m * 16 : m * 16 + 16, :] = sines[m] * factor
    for s in range(SLOTS):
        got = basrow[pl.ds(s, 8, stride=16), :]
        bas[0:8, lanes(s)] = got
        bas[8:16, lanes(s)] = got - got.astype(bf16).astype(f32)


def geometry_back(geo, dyref, dbas):
    (x, y, z), d, rd, env, slope, sines, cosines = geo
    g = [dyref[k * 16 : k * 16 + 16, :] for k in range(8)]
    dx = R3 * g[0] + R15 * (y * g[3] + z * g[6] + x * g[7]) - R5 * x * g[5]
    dy = R3 * g[1] + R15 * (x * g[3] + z * g[4] - y * g[7]) - R5 * y * g[5]
    dz = R3 * g[2] + R15 * (y * g[4] + x * g[6]) + 2.0 * R5 * z * g[5]
    along = jnp.zeros_like(x)
    turned = jnp.zeros_like(x)
    for m in range(8):
        db = dbas[m * 16 : m * 16 + 16, :]
        along = along + db * sines[m]
        turned = turned + ((m + 1) * math.pi / RADIUS) * db * cosines[m]
    dd = SCALE * rd * (turned * env + along * (slope - env * rd))
    dd = dd - (dx * x + dy * y + dz * z) * rd
    return dx * rd + x * dd, dy * rd + y * dd, dz * rd + z * dd


def radial_forward(bas, first, second, third, wref, e1=None, e2=None):
    pre = mm(first[...], bas[...].astype(bf16))
    h, e = silu_parts(pre[:HID] + pre[HID:])
    if e1 is not None:
        e1[...] = e
    h, e = silu_parts(mm(second[...], split3(h)))
    if e2 is not None:
        e2[...] = e
    h = split3(h)
    for p in range(third.shape[0] // CH):
        wref[p * CH : (p + 1) * CH, :] = mm(third[p * CH : (p + 1) * CH, :], h)


def radial_back(dwref, third_t, second_t, first_t, e1, e2, dbrow, dbas):
    both = mm(third_t[...], dwref[...])
    dp = (both[:HID] + both[HID:]) * e2[...]
    dp = mm(second_t[...], split3(dp)) * e1[...]
    dbrow[...] = mm(first_t[...], split3(dp))
    dbas[...] = jnp.zeros_like(dbas)
    for s in range(SLOTS):
        dbas[pl.ds(s, 8, stride=16), :] = dbrow[0:8, lanes(s)]


ORDERS = ((0, 1), (1, 3), (4, 5))


def mixed(matrices, values, out):
    for l, (start, n) in enumerate(ORDERS):
        out[:, lanes(start, n)] = mm(matrices[l], split3(values[:, lanes(start, n)]))


def sum_of(terms):
    total = terms[0]
    for t in terms[1:]:
        total = total + t
    return total


def first_features(geo, emb, fref):
    iota = lax.broadcasted_iota(jnp.int32, (CH, LANES), 0)
    for s in range(SLOTS):
        kind = geo[0, 48 + s : 49 + s, :].astype(jnp.int32)
        hot = (iota == kind).astype(f32).astype(bf16)
        both = mm(emb[...], hot)
        fref[:, lanes(s)] = both[:CH] + both[CH:]


def layer_one_kernel(geo, kinds, first, second, third, emb, mf, mo, coef, out, keep, yref, basrow, bas, wref, fref, aref):
    place_geometry(geometry(geo[0, 0:16, :], geo[0, 16:32, :], geo[0, 32:48, :]), yref, basrow, bas)
    radial_forward(bas, first, second, third, wref)
    first_features(geo, emb, fref)

    def messages(c, _):
        acc = [None] * 9

        def add(k, v):
            acc[k] = v if acc[k] is None else acc[k] + v

        r0 = pl.ds(pl.multiple_of(c * 16, 16), 16)
        r1 = pl.ds(pl.multiple_of(c * 16 + CH, 16), 16)
        r2 = pl.ds(pl.multiple_of(c * 16 + 2 * CH, 16), 16)
        for s in range(SLOTS):
            f = fref[r0, lanes(s)]
            add(0, wref[r0, lanes(s)] * f)
            w1 = wref[r1, lanes(s)] * f
            w2 = wref[r2, lanes(s)] * f
            for k in range(8):
                add(k + 1, (w1 if k < 3 else w2) * yref[k * 16 + s : k * 16 + s + 1, :])
        for k in range(9):
            aref[r0, lanes(k)] = acc[k] * (1.0 / SLOTS)
        return 0

    lax.fori_loop(0, CH // 16, messages, 0)
    mixed(mf, aref, keep.at[0])
    p = [keep[0, :, lanes(k)] for k in range(9)]
    c = [coef[:, k : k + 1] for k in range(5)]
    aref[:, lanes(0)] = (
        p[0]
        + c[0] * p[0] * p[0]
        + c[1] * sum_of([p[k] * p[k] for k in range(1, 4)])
        + c[2] * sum_of([p[k] * p[k] for k in range(4, 9)])
    )
    up, ut = 1.0 + c[3] * p[0], 1.0 + c[4] * p[0]
    for k in range(1, 9):
        aref[:, lanes(k)] = p[k] * (up if k < 4 else ut)
    iota = lax.broadcasted_iota(jnp.int32, (CH, LANES), 0)
    hot = (iota == kinds[...].astype(jnp.int32)).astype(f32).astype(bf16)
    both = mm(emb[...], hot)
    out[0:CH, :] = (mm(mo[0], split3(aref[:, lanes(0)])) + (both[:CH] + both[CH:])).astype(bf16)
    for l, (start, n) in enumerate(ORDERS[1:], 1):
        got = mm(mo[l], split3(aref[:, lanes(start, n)]))
        for k in range(n):
            out[(start + k) * CH : (start + k + 1) * CH, :] = got[:, lanes(k)].astype(bf16)


def whole(a):
    rank = len(a.shape)
    return pl.BlockSpec(a.shape, lambda i: (0,) * rank)


def layer_one(geo, kinds, start, weights):
    n = geo.shape[0]
    first, second, third = weights["r1"]
    consts = (first, second, third, weights["emb"], weights["mf1"], weights["of1"], weights["coef1"])
    return call(
        layer_one_kernel,
        (shape(9 * CH, n * LANES, kind=bf16), shape(n, CH, 9 * LANES)),
        grid=(n,),
        in_specs=[
            pl.BlockSpec((1, 64, LANES), lambda i: (i, 0, 0)),
            pl.BlockSpec((1, LANES), lambda i: (0, i + start)),
        ]
        + [whole(a) for a in consts],
        out_specs=(
            pl.BlockSpec((9 * CH, LANES), lambda i: (0, i)),
            pl.BlockSpec((1, CH, 9 * LANES), lambda i: (i, 0, 0)),
        ),
        scratch=[
            pltpu.VMEM((128, LANES), f32),
            pltpu.VMEM((128, LANES), f32),
            pltpu.VMEM((16, EDGES), f32),
            pltpu.VMEM((3 * CH, EDGES), f32),
            pltpu.VMEM((CH, EDGES), f32),
            pltpu.VMEM((CH, 9 * LANES), f32),
        ],
        flops=n * 900000000,
    )(geo, kinds, *consts)


def layer_one_back_kernel(
    geo, grad, keep, first, second, third, third_t, second_t, first_t, emb, mb, mo, coef,
    out, yref, basrow, bas, wref, fref, aref, dref, e1, e2, dwref, dyref, dbrow, dbas,
):
    geom = geometry(geo[0, 0:16, :], geo[0, 16:32, :], geo[0, 32:48, :])
    place_geometry(geom, yref, basrow, bas)
    radial_forward(bas, first, second, third, wref, e1, e2)
    first_features(geo, emb, fref)
    for k in range(9):
        aref[:, lanes(k)] = grad[k * CH : (k + 1) * CH, :]
    mixed(mo, aref, dref)
    p = [keep[0, :, lanes(k)] for k in range(9)]
    g = [dref[:, lanes(k)] for k in range(9)]
    c = [coef[:, k : k + 1] for k in range(5)]
    aref[:, lanes(0)] = (
        g[0] * (1.0 + 2.0 * c[0] * p[0])
        + c[3] * sum_of([p[k] * g[k] for k in range(1, 4)])
        + c[4] * sum_of([p[k] * g[k] for k in range(4, 9)])
    )
    up, ut = 1.0 + c[3] * p[0], 1.0 + c[4] * p[0]
    vp, vt = 2.0 * c[1] * g[0], 2.0 * c[2] * g[0]
    for k in range(1, 9):
        aref[:, lanes(k)] = g[k] * (up if k < 4 else ut) + p[k] * (vp if k < 4 else vt)
    mixed(mb, aref, dref)
    dref[...] = dref[...] * (1.0 / SLOTS)
    dyref[...] = jnp.zeros_like(dyref)

    def slot(s, _):
        here = pl.ds(pl.multiple_of(s * LANES, LANES), LANES)
        y = [yref[pl.ds(k * 16 + s, 1), :] for k in range(8)]
        dy = [None] * 8
        for c in range(CH // 16):
            r0, r1, r2 = (slice(q * CH + c * 16, q * CH + c * 16 + 16) for q in range(3))
            f = fref[r0, here]
            w1 = wref[r1, here] * f
            w2 = wref[r2, here] * f
            d = [dref[r0, lanes(k)] for k in range(9)]
            dwref[r0, here] = (d[0] * f).astype(bf16)
            dwref[r1, here] = (f * sum_of([d[k + 1] * y[k] for k in range(3)])).astype(bf16)
            dwref[r2, here] = (f * sum_of([d[k + 1] * y[k] for k in range(3, 8)])).astype(bf16)
            for k in range(8):
                v = (w1 if k < 3 else w2) * d[k + 1]
                v = v[0:8] + v[8:16]
                dy[k] = v if dy[k] is None else dy[k] + v
        for k in range(8):
            dyref[pl.ds(k * 16 + s, 1), :] = jnp.sum(dy[k], axis=0, keepdims=True)
        return 0

    lax.fori_loop(0, SLOTS, slot, 0)
    radial_back(dwref, third_t, second_t, first_t, e1, e2, dbrow, dbas)
    dx, dy, dz = geometry_back(geom, dyref, dbas)
    out[0, 0:16, :] = dx
    out[0, 16:32, :] = dy
    out[0, 32:48, :] = dz


def layer_one_back(geo, grad, start, keep, weights):
    n = geo.shape[0]
    first, second, third = weights["r1"]
    consts = (first, second, third) + weights["b1"] + (
        weights["emb"], weights["mb1"], weights["ob1"], weights["coef1"])
    return call(
        layer_one_back_kernel,
        shape(n, 48, LANES),
        grid=(n,),
        in_specs=[
            pl.BlockSpec((1, 64, LANES), lambda i: (i, 0, 0)),
            pl.BlockSpec((9 * CH, LANES), lambda i: (0, i + start)),
            pl.BlockSpec((1, CH, 9 * LANES), lambda i: (i, 0, 0)),
        ]
        + [whole(a) for a in consts],
        out_specs=pl.BlockSpec((1, 48, LANES), lambda i: (i, 0, 0)),
        scratch=[
            pltpu.VMEM((128, LANES), f32),
            pltpu.VMEM((128, LANES), f32),
            pltpu.VMEM((16, EDGES), f32),
            pltpu.VMEM((3 * CH, EDGES), f32),
            pltpu.VMEM((CH, EDGES), f32),
            pltpu.VMEM((CH, 9 * LANES), f32),
            pltpu.VMEM((CH, 9 * LANES), f32),
            pltpu.VMEM((HID, EDGES), f32),
            pltpu.VMEM((HID, EDGES), f32),
            pltpu.VMEM((3 * CH, EDGES), bf16),
            pltpu.VMEM((128, LANES), f32),
            pltpu.VMEM((16, EDGES), f32),
            pltpu.VMEM((128, LANES), f32),
        ],
        flops=n * 2000000000,
    )(geo, grad, keep, *consts)


def build_hot(vcol, b, hot):
    iota = lax.broadcasted_iota(jnp.int32, (COLS, LANES), 0)

    def one(s, _):
        v = vcol[b, pl.ds(s, 1), :]
        hot[:, pl.ds(pl.multiple_of(s * LANES, LANES), LANES)] = (iota == v).astype(f32).astype(bf16)
        return 0

    lax.fori_loop(0, SLOTS, one, 0)


def layer_two_kernel(
    tl, tx, ty, geo, vcol, occ, first, second, third, third_t, second_t, first_t, mf, mb, of, ob,
    coef, lin, rh, rht, ro, energy, dtab, dgeo,
    tab, yref, basrow, bas, wref, aref, dref, e1, e2, dwref, dyref, dbrow, dbas, hot, gat, dgat,
):
    tab[:, 0:384] = tl[...]
    tab[:, 384:640] = tx[...]
    tab[:, 640:1408] = ty[...]
    dtab[...] = jnp.zeros_like(dtab)
    dyref[...] = jnp.zeros_like(dyref)

    def block(b, _):
        rows16 = lambda k: geo[b, k * 16 : k * 16 + 16, :]
        geom = geometry(rows16(0), rows16(1), rows16(2))
        place_geometry(geom, yref, basrow, bas)
        radial_forward(bas, first, second, third, wref, e1, e2)
        build_hot(vcol, b, hot)

        def gather(j, _):
            here = pl.ds(pl.multiple_of(j * 256, 256), 256)
            gat[:, here] = mm(tab[...], hot[:, here]).astype(bf16)
            return 0

        lax.fori_loop(0, EDGES // 256, gather, 0)

        def messages(c, _):
            acc = [None] * 9

            def add(k, v):
                acc[k] = v if acc[k] is None else acc[k] + v

            r = [pl.ds(pl.multiple_of(c * 16 + q * CH, 16), 16) for q in range(9)]
            for s in range(SLOTS):
                y = [yref[k * 16 + s : k * 16 + s + 1, :] for k in range(8)]
                x = [gat[r[q], lanes(s)].astype(f32) for q in range(9)]
                w = [wref[r[q], lanes(s)] for q in range(7)]
                a1 = sum_of([y[k] * x[k + 1] for k in range(3)])
                a2 = sum_of([y[k] * x[k + 1] for k in range(3, 8)])
                add(0, w[0] * x[0] + w[1] * a1 + w[2] * a2)
                t1, t2 = w[3] * x[0], w[5] * x[0]
                for k in range(8):
                    add(k + 1, (t1 if k < 3 else t2) * y[k] + (w[4] if k < 3 else w[6]) * x[k + 1])
            for k in range(9):
                aref[r[0], lanes(k)] = acc[k] * (1.0 / SLOTS)
            return 0

        lax.fori_loop(0, CH // 16, messages, 0)
        mixed(mf, aref, dref)
        p = [dref[:, lanes(k)] for k in range(9)]
        c = [coef[:, k : k + 1] for k in range(3)]
        prod = (
            p[0]
            + c[0] * p[0] * p[0]
            + c[1] * sum_of([p[k] * p[k] for k in range(1, 4)])
            + c[2] * sum_of([p[k] * p[k] for k in range(4, 9)])
        )
        ownl = pl.ds(pl.multiple_of(b * LANES, LANES), LANES)
        base = tab[0:CH, ownl].astype(f32)
        scal = mm(of[...], split3(prod)) + base
        h, e = silu_parts(mm(rht[...], split3(scal)))
        mask = occ[:, ownl]
        tot = jnp.sum(ro[...] * h, axis=0, keepdims=True) + jnp.sum(lin[...] * base, axis=0, keepdims=True)
        energy[:, ownl] = tot * mask
        ds = mm(rh[...], split3(ro[...] * e * mask))
        dtab[0:CH, ownl] = dtab[0:CH, ownl] + ds + lin[...] * mask
        db = mm(ob[...], split3(ds))
        aref[:, lanes(0)] = db * (1.0 + 2.0 * c[0] * p[0])
        for k in range(1, 9):
            aref[:, lanes(k)] = 2.0 * (c[1] if k < 4 else c[2]) * p[k] * db
        mixed(mb, aref, dref)
        dref[...] = dref[...] * (1.0 / SLOTS)

        def slot(s, _):
            here = pl.ds(pl.multiple_of(s * LANES, LANES), LANES)
            y = [yref[pl.ds(k * 16 + s, 1), :] for k in range(8)]
            dy = [None] * 8
            for cc in range(CH // 16):
                r = [slice(q * CH + cc * 16, q * CH + cc * 16 + 16) for q in range(9)]
                x = [gat[r[q], here].astype(f32) for q in range(9)]
                w = [wref[r[q], here] for q in range(7)]
                d = [dref[r[0], lanes(k)] for k in range(9)]
                t1 = sum_of([y[k] * d[k + 1] for k in range(3)])
                t2 = sum_of([y[k] * d[k + 1] for k in range(3, 8)])
                a1 = sum_of([y[k] * x[k + 1] for k in range(3)])
                a2 = sum_of([y[k] * x[k + 1] for k in range(3, 8)])
                b1 = sum_of([d[k + 1] * x[k + 1] for k in range(3)])
                b2 = sum_of([d[k + 1] * x[k + 1] for k in range(3, 8)])
                dgat[r[0], here] = (w[0] * d[0] + w[3] * t1 + w[5] * t2).astype(bf16)
                m1, m2 = w[1] * d[0], w[2] * d[0]
                n1, n2 = w[3] * x[0], w[5] * x[0]
                for k in range(8):
                    m, n, q = (m1, n1, w[4]) if k < 3 else (m2, n2, w[6])
                    dgat[r[k + 1], here] = (m * y[k] + q * d[k + 1]).astype(bf16)
                    v = m * x[k + 1] + n * d[k + 1]
                    v = v[0:8] + v[8:16]
                    dy[k] = v if dy[k] is None else dy[k] + v
                for q, v in enumerate((d[0] * x[0], d[0] * a1, d[0] * a2, x[0] * t1, b1, x[0] * t2, b2)):
                    dwref[r[q], here] = v.astype(bf16)
            for k in range(8):
                dyref[pl.ds(k * 16 + s, 1), :] = jnp.sum(dy[k], axis=0, keepdims=True)
            return 0

        lax.fori_loop(0, SLOTS, slot, 0)

        def scatter(j, _):
            here = pl.ds(pl.multiple_of(j * 256, 256), 256)
            dtab[:, here] = dtab[:, here] + mm_nt(dgat[...], hot[here, :])
            return 0

        lax.fori_loop(0, COLS // 256, scatter, 0)
        rest = COLS // 256 * 256
        dtab[:, rest:COLS] = dtab[:, rest:COLS] + mm_nt(dgat[...], hot[rest:COLS, :])
        radial_back(dwref, third_t, second_t, first_t, e1, e2, dbrow, dbas)
        dx, dy, dz = geometry_back(geom, dyref, dbas)
        dgeo[b, 0:16, :] = dx
        dgeo[b, 16:32, :] = dy
        dgeo[b, 32:48, :] = dz
        return 0

    lax.fori_loop(0, LOCAL, block, 0)


def layer_two(tl, tx, ty, geo, vcol, occ, w):
    first, second, third = w["r2"]
    return call(
        layer_two_kernel,
        (shape(1, LOCAL * LANES), shape(9 * CH, COLS), shape(LOCAL, 48, LANES)),
        scratch=[
            pltpu.VMEM((9 * CH, COLS), bf16),
            pltpu.VMEM((128, LANES), f32),
            pltpu.VMEM((128, LANES), f32),
            pltpu.VMEM((16, EDGES), f32),
            pltpu.VMEM((7 * CH, EDGES), f32),
            pltpu.VMEM((CH, 9 * LANES), f32),
            pltpu.VMEM((CH, 9 * LANES), f32),
            pltpu.VMEM((HID, EDGES), f32),
            pltpu.VMEM((HID, EDGES), f32),
            pltpu.VMEM((7 * CH, EDGES), bf16),
            pltpu.VMEM((128, LANES), f32),
            pltpu.VMEM((16, EDGES), f32),
            pltpu.VMEM((128, LANES), f32),
            pltpu.VMEM((COLS, EDGES), bf16),
            pltpu.VMEM((9 * CH, EDGES), bf16),
            pltpu.VMEM((9 * CH, EDGES), bf16),
        ],
        flops=40000000000,
    )(tl, tx, ty, geo, vcol, occ, first, second, third, *w["b2"], w["mf2"], w["mb2"], w["of2"],
      w["ob2"], w["coef2"], w["lin"], w["rh"], w["rht"], w["ro"])


def split_rows(x):
    hi = x.astype(bf16).astype(f32)
    rest = x - hi
    mid = rest.astype(bf16).astype(f32)
    return hi, mid, rest - mid


def place_border(x, border):
    slots = lax.broadcasted_iota(jnp.int32, (2 * LANES, LANES), 0)
    hot = (slots == border[...]).astype(f32).astype(bf16)
    n = x.shape[0]
    got = mm_nt(jnp.concatenate(split_rows(x), axis=0).astype(bf16), hot)
    return got[:n] + got[n : 2 * n] + got[2 * n :]


def columns_kernel(g2, g1, b0, b1, b2, b3, vcol, border, out, tot, lhs, hot):
    tot[...] = jnp.zeros_like(tot)
    for b in range(LOCAL):
        tot[b, 0:48, :] = g2[b] + g1[b]
    placed = place_border(b0[...] + b1[...] + (b2[...] + b3[...]), border)
    for b in range(2):
        tot[b, 0:48, :] = tot[b, 0:48, :] + placed[:, lanes(b)]
    out[...] = jnp.zeros_like(out)

    def block(b, _):
        build_hot(vcol, b, hot)
        lhs[...] = jnp.zeros_like(lhs)
        own = jnp.zeros((4, LANES), f32)
        for s in range(SLOTS):
            x = tot[b, pl.ds(s, 4, stride=16), :]
            own = own + x
            for q, part in enumerate(split_rows(x)):
                lhs[q * 8 : q * 8 + 4, lanes(s)] = part
        got = mm_nt(lhs[...].astype(bf16), hot[...])
        out[...] = out[...] + (got[0:8] + got[8:16] + got[16:24])
        ownl = pl.ds(pl.multiple_of(b * LANES, LANES), LANES)
        out[0:4, ownl] = out[0:4, ownl] - own
        return 0

    lax.fori_loop(0, LOCAL, block, 0)


def forces_kernel(col, r1, r2, xp, xn, border, out):
    total = xp[...] + xn[...] + (r1[:, lanes(1)] + r2[:, lanes(1)])
    placed = place_border(total, border)
    out[:, 0:256] = -(col[0:3, 0:256] + placed[0:3])
    out[:, 256:384] = -col[0:3, 256:384]


def from_behind(block, axis, distance):
    count = lax.axis_size(axis)
    route = [((i - distance) % count, i) for i in range(count)]
    return lax.ppermute(block, axis, route)


def rounded(x):
    hi = lax.reduce_precision(x, 8, 7)
    return hi.astype(bf16), (x - hi).astype(bf16)


def left3(x):
    hi, lo = rounded(x)
    return jnp.concatenate([hi, hi, lo], axis=-1)


def prepare(embedding, radial_in, radial_mid, outs, mix, mix_out_one, mix_out_two, product_one, product_two, read_lin, read_hidden, read_out):
    w = {}
    for t in range(2):
        hi, lo = rounded(radial_in[t].T)
        first = jnp.concatenate(
            [jnp.concatenate([hi, hi], axis=1), jnp.concatenate([lo, jnp.zeros_like(lo)], axis=1)], axis=0)
        name = str(t + 1)
        w["r" + name] = (first, left3(radial_mid[t].T), left3(outs[t].T))
        back_in = jnp.concatenate([radial_in[t], jnp.zeros_like(radial_in[t])], axis=0)
        w["b" + name] = (jnp.concatenate(rounded(outs[t]), axis=0), left3(radial_mid[t]), left3(back_in))
        w["mf" + name] = left3(jnp.swapaxes(mix[t], 1, 2))
        w["mb" + name] = left3(mix[t])
    w["of1"] = left3(jnp.swapaxes(mix_out_one, 1, 2))
    w["ob1"] = left3(mix_out_one)
    w["of2"] = left3(mix_out_two.T)
    w["ob2"] = left3(mix_out_two)
    w["coef1"] = product_one.T
    w["coef2"] = product_two.T
    padded = jnp.pad(embedding, ((0, CH - embedding.shape[0]), (0, 0))).T
    w["emb"] = jnp.concatenate(rounded(padded), axis=0)
    w["lin"] = read_lin[:, None]
    w["rh"] = left3(read_hidden)
    w["rht"] = left3(read_hidden.T)
    w["ro"] = read_out[:, None]
    return w


def on_device(
    positions, species, dest_key, send_list, send_count, border, neighbours, embedding, radial_in,
    radial_mid, radial_out_one, radial_out_two, mix, mix_out_one, mix_out_two, product_one,
    product_two, read_lin, read_hidden, read_out,
):
    pos = positions[0, 0]
    spec = species[0]
    key = dest_key[0]
    rows = border[0]
    nbr = neighbours[0, 0].T
    packet = call(
        packet_kernel,
        shape(8, 256),
        scratch=[pltpu.VMEM((8, 256), f32)],
        in_specs=[VMEM, VMEM, VMEM, VMEM, SMEM],
    )(pos, spec, send_list.reshape(1, LANES), rows, send_count.reshape(4))
    xp = from_behind(packet, "gx", 1)
    xn = from_behind(packet, "gx", -1)
    wide = jnp.concatenate([packet, xp[:, LANES:], xn[:, LANES:]], axis=1)
    yp = from_behind(wide, "gy", 1)
    yn = from_behind(wide, "gy", -1)
    w = prepare(embedding, radial_in, radial_mid, (radial_out_one, radial_out_two), mix, mix_out_one,
                mix_out_two, product_one, product_two, read_lin, read_hidden, read_out)
    geo, bgeo, vcol, kinds, occ = call(
        edges_kernel,
        (
            shape(LOCAL, 64, LANES),
            shape(64, LANES),
            shape(LOCAL, 16, LANES, kind=jnp.int32),
            shape(1, COLS),
            shape(1, LOCAL * LANES),
        ),
        scratch=[pltpu.VMEM((8, COLS), f32)],
    )(pos, spec, key, xp, xn, yp, yn, nbr, rows)
    gxp = from_behind(bgeo, "gx", 1)
    gxn = from_behind(bgeo, "gx", -1)
    tl, kl = layer_one(geo, kinds, 0, w)
    three = jnp.stack([gxp, bgeo, gxn])
    gyp = from_behind(three, "gy", 1)
    gyn = from_behind(three, "gy", -1)
    geo_x = jnp.stack([gxp, gxn])
    tx, kx = layer_one(geo_x, kinds, 3, w)
    geo_y = jnp.concatenate([gyp, gyn], axis=0)
    ty, ky = layer_one(geo_y, kinds, 5, w)
    energy, dtab, g2 = layer_two(tl, tx, ty, geo, vcol, occ, w)
    dgy = layer_one_back(geo_y, dtab, 5, ky, w)
    ry1 = from_behind(dgy[0:3], "gy", -1)
    ry2 = from_behind(dgy[3:6], "gy", 1)
    dgx = layer_one_back(geo_x, dtab, 3, kx, w)
    rx1 = from_behind(dgx[0] + ry1[0] + ry2[0], "gx", -1)
    rx2 = from_behind(dgx[1] + ry1[2] + ry2[2], "gx", 1)
    g1 = layer_one_back(geo, dtab, 0, kl, w)
    col = call(
        columns_kernel,
        shape(8, COLS),
        scratch=[
            pltpu.VMEM((LOCAL, 64, LANES), f32),
            pltpu.VMEM((24, EDGES), f32),
            pltpu.VMEM((COLS, EDGES), bf16),
        ],
    )(g2, g1, ry1[1], ry2[1], rx1, rx2, vcol, rows)
    r1 = from_behind(col[:, 640:1024], "gy", -1)
    r2 = from_behind(col[:, 1024:1408], "gy", 1)
    sx1 = from_behind(col[:, 384:512] + r1[:, 0:128] + r2[:, 0:128], "gx", -1)
    sx2 = from_behind(col[:, 512:640] + r1[:, 256:384] + r2[:, 256:384], "gx", 1)
    forces = call(forces_kernel, shape(3, LOCAL * LANES))(col, r1, r2, sx1, sx2, rows)
    return energy[None], forces[None, None]


def solution(mesh):
    along = P("gx", "gy")
    in_specs = (along,) * 7 + (P(),) * 13
    return jax.shard_map(
        on_device, mesh=mesh, in_specs=in_specs, out_specs=(along, along), check_vma=False
    )
```

time: 1800 us -> 250 us (0.14)
  local copies, waits for them, and re-layouts: 894 us -> 18.8 us
  other arithmetic: 530 us -> 17.2 us
  matrix products: 213 us -> 0 us
  Pallas kernels: 0 us -> 172 us
  waiting for transfers between devices: 62.7 us -> 8.34 us
  loops' own time: 36.6 us -> 0 us
    gather x89 -> x0, local copies, waits for them, and re-layouts: 290 us -> none  [the longest x24 125 us: interaction(): source = feats_all[:, flat_index] * edge_mask[None, :]]
    dot_general x137 -> x0, matrix products: 213 us -> none  [the longest x78 98.4 us: contract(): return jnp.einsum('cd,...cn->...dn', matrix, values, precision=highest)]
    reduce_sum x84 -> x0, other arithmetic: 187 us -> none  [the longest x36 86.6 us: pooling(): jnp.sum(message.reshape(message.shape[:-1] + (atoms, slots)), axis=-1)]
    pallas_call x0 -> x11, Pallas kernels: none -> 172 us  [the longest x1 76.2 us: layer_two(): call(layer_two_kernel, (shape(1, LOCAL * LANES), shape(9 * CH, COLS), sha...]
    mul x132 -> x0, local copies, waits for them, and re-layouts: 151 us -> none  [the longest x3 24.2 us: interaction(): source = feats_all[:, flat_index] * edge_mask[None, :]]
    reshape x106 -> x1, local copies, waits for them, and re-layouts: 122 us -> 1.27 us  [on_device(): send_list.reshape(1, LANES)]
    scatter-add x12 -> x0, other arithmetic: 117 us -> none  [the longest x3 56.5 us: interaction(): source = feats_all[:, flat_index] * edge_mask[None, :]]
    mul x114 -> x0, other arithmetic: 108 us -> none  [the longest x9 32 us: interaction(): source = feats_all[:, flat_index] * edge_mask[None, :]]
  transfers between devices with their start and end apart: 20 -> 16, of which waited for: 11 -> 3; matrix products, arithmetic and copies ran while one was open for 2% -> 10% of each run, Pallas kernels for 0% -> 16%
where the time goes in v1:
time: 250 us; the launch traced here: 246 us
  Pallas kernels  172 us (69%)
  starting transfers between devices  28.7 us (11%)
  local copies, waits for them, and re-layouts  18.8 us (8%)
  other arithmetic  17.2 us (7%)
  waiting for transfers between devices  8.34 us (3%)
    pallas_call x1, Pallas kernels, layer_two(): call(layer_two_kernel, (shape(1, LOCAL * LANES), shape(9 * CH, COLS), sha...  76.2 us
    pallas_call x3, Pallas kernels, layer_one_back(): call(layer_one_back_kernel, shape(n, 48, LANES), grid=(n,), in_specs=[pl....  47.5 us
    pallas_call x3, Pallas kernels, layer_one(): call(layer_one_kernel, (shape(9 * CH, n * LANES, kind=bf16), shape(n, CH,...  33.5 us
    ppermute x16, starting transfers between devices, from_behind(): return lax.ppermute(block, axis, route)  28.7 us
    pallas_call x1, Pallas kernels, on_device(): call(columns_kernel, shape(8, COLS), scratch=[pltpu.VMEM((LOCAL, 64, LANE...  9.32 us
    unnamed x61, local copies, waits for them, and re-layouts  8.43 us
    ppermute x16, waiting for transfers between devices, from_behind(): return lax.ppermute(block, axis, route)  8.34 us
    concatenate x16, other arithmetic, left3(): return jnp.concatenate([hi, hi, lo], axis=-1)  8.3 us
  transfers between devices with their start and end apart: 16, of which 3 were waited for; matrix products, arithmetic and copies ran while one was open for 10% of the time, Pallas kernels for 16%

profile of v1, /device:TPU:26, one launch (start us, length us, event | category | flops | bytes accessed | tf_op | source)
XLA Modules:
  0.0 245.9 jit_solution(15924631034728606086)
XLA Ops:
  0.7 1.3 copy.86
  3.3 1.5 shard_map.203
  4.9 1.9 collective-permute-start.1
  23.0 5.3 %collective-permute-start.3 = (f32[8,512]{1,0:T(8,128)S(1)}, f32[8,512]{1,0:T(8,128)S(1)}, u32[]{:S(2)}, u32[]{:S(2)}) collective-permute-start(f32[8,512]{1,0:T(8,128)S(1)} %pad_maximum_fusion.19), channel_id=1, source_target_pairs={{1,0},{2,1},{3,2},{4,3},{5,4},{6,5},{7,6},{8,7},{9,8},{10,9},{11,1... | collective-permute-start | bytes 49160 | tf_op jit(solution)/shard_map/ppermute | solution.py:660
  37.8 2.1 shard_map.204
  40.0 2.4 collective-permute-start.4
  42.4 9.5 %shard_map.205 = (bf16[1152,384]{1,0:T(8,128)(2,1)}, f32[3,128,1152]{2,1,0:T(8,128)}) custom-call(f32[3,64,128]{2,1,0:T(8,128)} %get-tuple-element.16.geo, f32[1,1408]{1,0:T(1,128)} %get-tuple-element.17.kinds, bf16[128,16]{1,0:T(8,128)(2,1)} %copy.56.first, bf16[64,192]{1,0:T(8,128)(2,1)} %copy.57.second, bf16[384,192]{1,0:T(8,128)(2,1)} %pad_maximum_fusion.8.third, ...), custom_call_target="tpu_custom_call" | custom-call | flops 2700000000 | bytes 1000000 | tf_op jit(solution)/shard_map/pallas_call | solution.py:331
  52.0 5.3 %collective-permute-start.7 = (f32[3,64,128]{2,1,0:T(8,128)S(1)}, f32[3,64,128]{2,1,0:T(8,128)S(1)}, u32[]{:S(2)}, u32[]{:S(2)}) collective-permute-start(f32[3,64,128]{2,1,0:T(8,128)S(1)} %pad_maximum_fusion.9), channel_id=1, source_target_pairs={{1,0},{2,1},{3,2},{4,3},{5,4},{6,5},{7,6},{8,7},{9,8},{10,9},{11,1... | collective-permute-start | bytes 294920 | tf_op jit(solution)/shard_map/ppermute | solution.py:660
  58.0 6.9 %shard_map.206 = (bf16[1152,256]{1,0:T(8,128)(2,1)}, f32[2,128,1152]{2,1,0:T(8,128)}) custom-call(f32[2,64,128]{2,1,0:T(8,128)} %pad_maximum_fusion.14.geo, f32[1,1408]{1,0:T(1,128)} %get-tuple-element.17.kinds, bf16[128,16]{1,0:T(8,128)(2,1)} %copy.56.first, bf16[64,192]{1,0:T(8,128)(2,1)} %copy.57.second, bf16[384,192]{1,0:T(8,128)(2,1)} %pad_maximum_fusion.8.third, ...), custom_call_target="tpu_custom_call" | custom-call | flops 1800000000 | bytes 1000000 | tf_op jit(solution)/shard_map/pallas_call | solution.py:331
  65.6 17.0 %shard_map.207 = (bf16[1152,768]{1,0:T(8,128)(2,1)}, f32[6,128,1152]{2,1,0:T(8,128)}) custom-call(f32[6,64,128]{2,1,0:T(8,128)} %copy-done.6, f32[1,1408]{1,0:T(1,128)} %get-tuple-element.17.kinds, bf16[128,16]{1,0:T(8,128)(2,1)} %copy.56.first, bf16[64,192]{1,0:T(8,128)(2,1)} %copy.57.second, bf16[384,192]{1,0:T(8,128)(2,1)} %pad_maximum_fusion.8.third, ...), custom_call_target="tpu_custom_call" | custom-call | flops 5400000000 | bytes 1000000 | tf_op jit(solution)/shard_map/pallas_call | solution.py:331
  82.7 76.2 %shard_map.208 = (f32[1,384]{1,0:T(1,128)}, f32[1152,1408]{1,0:T(8,128)}, f32[3,48,128]{2,1,0:T(8,128)}) custom-call(bf16[1152,384]{1,0:T(8,128)(2,1)} %get-tuple-element.18.tl, bf16[1152,256]{1,0:T(8,128)(2,1)} %get-tuple-element.20.tx, bf16[1152,768]{1,0:T(8,128)(2,1)} %get-tuple-element.21.ty, f32[3,64,128]{2,1,0:T(8,128)} %get-tuple-element.16.geo, ...), custom_call_target="tpu_custom_call" | custom-call | flops 40000000000 | bytes 1000000 | tf_op jit(solution)/shard_map/pallas_call | solution.py:582
  158.8 24.4 %shard_map.210 = f32[6,48,128]{2,1,0:T(8,128)} custom-call(f32[6,64,128]{2,1,0:T(8,128)} %copy-done.6, f32[1152,1408]{1,0:T(8,128)} %get-tuple-element.26.grad, f32[6,128,1152]{2,1,0:T(8,128)} %get-tuple-element.28.keep, bf16[128,16]{1,0:T(8,128)(2,1)} %copy.56.first, bf16[64,192]{1,0:T(8,128)(2,1)} %copy.57.second, ...), custom_call_target="tpu_custom_call" | custom-call | flops 12000000000 | bytes 1000000 | tf_op jit(solution)/shard_map/pallas_call | solution.py:417
  185.0 9.7 %shard_map.211 = f32[2,48,128]{2,1,0:T(8,128)} custom-call(f32[2,64,128]{2,1,0:T(8,128)} %pad_maximum_fusion.14.geo, f32[1152,1408]{1,0:T(8,128)} %get-tuple-element.26.grad, f32[2,128,1152]{2,1,0:T(8,128)} %get-tuple-element.29.keep, bf16[128,16]{1,0:T(8,128)(2,1)} %copy.56.first, bf16[64,192]{1,0:T(8,128)(2,1)} %copy.57.second, ...), custom_call_target="tpu_custom_call" | custom-call | flops 4000000000 | bytes 1000000 | tf_op jit(solution)/shard_map/pallas_call | solution.py:417
  194.7 1.4 fusion.17
  196.1 2.1 collective-permute-start.10
  198.2 2.1 collective-permute-start.11
  200.3 13.4 %shard_map.209.g1 = f32[3,48,128]{2,1,0:T(8,128)} custom-call(f32[3,64,128]{2,1,0:T(8,128)} %get-tuple-element.16.geo, f32[1152,1408]{1,0:T(8,128)} %get-tuple-element.26.grad, f32[3,128,1152]{2,1,0:T(8,128)} %get-tuple-element.27.keep, bf16[128,16]{1,0:T(8,128)(2,1)} %copy.56.first, bf16[64,192]{1,0:T(8,128)(2,1)} %copy.57.second, ...), custom_call_target="tpu_custom_call" | custom-call | flops 6000000000 | bytes 1000000 | tf_op jit(solution)/shard_map/pallas_call | solution.py:417
  214.3 9.3 %shard_map.212.col = f32[8,1408]{1,0:T(8,128)} custom-call(f32[3,48,128]{2,1,0:T(8,128)} %get-tuple-element.25.g2, f32[3,48,128]{2,1,0:T(8,128)} %shard_map.209.g1, f32[48,128]{1,0:T(8,128)} %get-tuple-element.58.b0, f32[48,128]{1,0:T(8,128)} %get-tuple-element.59.b1, f32[48,128]{1,0:T(8,128)} %copy-done.12, f32[48,128]{1,0:T(8,128)} %copy-done.13, ...), custom_call_target="tpu_custom_call" | custom-call | flops 1000000 | bytes 1000000 | tf_op jit(solution)/shard_map/pallas_call | solution.py:752
  224.3 4.3 %collective-permute-start.12 = (f32[8,384]{1,0:T(8,128)S(1)}, f32[8,384]{1,0:T(8,128)S(1)}, u32[]{:S(2)}, u32[]{:S(2)}) collective-permute-start(f32[8,384]{1,0:T(8,128)S(1)} %get-tuple-element.77), channel_id=1, source_target_pairs={{1,0},{2,1},{3,2},{4,3},{5,4},{6,5},{7,6},{8,7},{9,8},{10,9},{11,1... | collective-permute-start | bytes 36872 | tf_op jit(solution)/shard_map/ppermute | solution.py:660
  228.7 1.4 collective-permute-done.12.r1
  230.1 5.3 %collective-permute-done.13.r2 = f32[8,384]{1,0:T(8,128)S(1)} collective-permute-done((f32[8,384]{1,0:T(8,128)S(1)}, f32[8,384]{1,0:T(8,128)S(1)}, u32[]{:S(2)}, u32[]{:S(2)}) %collective-permute-start.13) | collective-permute-done | bytes 12320 | tf_op jit(solution)/shard_map/ppermute | solution.py:660
  236.1 4.1 %collective-permute-start.15 = (f32[8,128]{1,0:T(8,128)S(1)}, f32[8,128]{1,0:T(8,128)S(1)}, u32[]{:S(2)}, u32[]{:S(2)}) collective-permute-start(f32[8,128]{1,0:T(8,128)S(1)} %get-tuple-element.60), channel_id=1, source_target_pairs={{112,0},{0,16},{16,32},{32,48},{48,64},{64,80},{80,96},{96,112},{1... | collective-permute-start | bytes 12296 | tf_op jit(solution)/shard_map/ppermute | solution.py:660
  240.3 1.6 collective-permute-done.14.xp
  243.0 1.6 shard_map.213
  (139 shorter events, 34.4 us)
Async XLA Ops:
  4.8 18.0 %collective-permute-start = (f32[8,256]{1,0:T(8,128)}, f32[8,256]{1,0:T(8,128)S(1)}, u32[]{:S(2)}, u32[]{:S(2)}) collective-permute-start(f32[8,256]{1,0:T(8,128)} %shard_map.203), channel_id=1, source_target_pairs={{112,0},{0,16},{16,32},{32,48},{48,64},{64,80},{80,96},{96,112},{1... | collective-permute-start | bytes 24584 | tf_op jit(solution)/shard_map/ppermute | solution.py:660
  4.9 17.9 %collective-permute-start.1 = (f32[8,256]{1,0:T(8,128)}, f32[8,256]{1,0:T(8,128)S(1)}, u32[]{:S(2)}, u32[]{:S(2)}) collective-permute-start(f32[8,256]{1,0:T(8,128)} %shard_map.203), channel_id=1, source_target_pairs={{16,0},{32,16},{48,32},{64,48},{80,64},{96,80},{112,96},{0,112},{1... | collective-permute-start | bytes 24584 | tf_op jit(solution)/shard_map/ppermute | solution.py:660
  15.4 13.0 %copy-start.16 = (s32[1,1,384,12]{2,1,3,0:T(1,128)S(1)}, s32[1,1,384,12]{2,1,3,0:T(1,128)}, u32[]{:S(2)}) copy-start(s32[1,1,384,12]{2,1,3,0:T(1,128)} %param.26) | copy-start | bytes 55300
  16.8 14.5 %copy-start.19 = (f32[5,128]{1,0:T(8,128)S(1)}, f32[5,128]{1,0:T(8,128)}, u32[]{:S(2)}) copy-start(f32[5,128]{1,0:T(8,128)} %param.35) | copy-start | bytes 7684
  18.5 16.6 %copy-start.22 = (f32[3,128]{1,0:T(4,128)S(1)}, f32[3,128]{1,0:T(4,128)}, u32[]{:S(2)}) copy-start(f32[3,128]{1,0:T(4,128)} %param.36) | copy-start | bytes 4612
  18.5 17.3 %copy-start.23 = (f32[128]{0:T(128)S(1)}, f32[128]{0:T(128)}, u32[]{:S(2)}) copy-start(f32[128]{0:T(128)} %param.37) | copy-start | bytes 1540
  18.5 18.0 %copy-start.24 = (f32[16]{0:T(128)S(1)}, f32[16]{0:T(128)}, u32[]{:S(2)}) copy-start(f32[16]{0:T(128)} %param.39) | copy-start | bytes 196
  22.8 14.4 %copy-start.14 = (f32[8,256]{1,0:T(8,128)}, f32[8,256]{1,0:T(8,128)S(1)}, u32[]{:S(2)}) copy-start(f32[8,256]{1,0:T(8,128)S(1)} %collective-permute-done.xp) | copy-start | bytes 24580
  22.8 14.4 %copy-start.15 = (f32[8,256]{1,0:T(8,128)}, f32[8,256]{1,0:T(8,128)S(1)}, u32[]{:S(2)}) copy-start(f32[8,256]{1,0:T(8,128)S(1)} %collective-permute-done.1.xn) | copy-start | bytes 24580
  22.9 14.4 %collective-permute-start.2 = (f32[8,512]{1,0:T(8,128)S(1)}, f32[8,512]{1,0:T(8,128)S(1)}, u32[]{:S(2)}, u32[]{:S(2)}) collective-permute-start(f32[8,512]{1,0:T(8,128)S(1)} %pad_maximum_fusion.19), channel_id=1, source_target_pairs={{15,0},{0,1},{1,2},{2,3},{3,4},{4,5},{5,6},{6,7},{7,8},{8,9},{9,10... | collective-permute-start | bytes 49160 | tf_op jit(solution)/shard_map/ppermute | solution.py:660
  23.0 14.3 %collective-permute-start.3 = (f32[8,512]{1,0:T(8,128)S(1)}, f32[8,512]{1,0:T(8,128)S(1)}, u32[]{:S(2)}, u32[]{:S(2)}) collective-permute-start(f32[8,512]{1,0:T(8,128)S(1)} %pad_maximum_fusion.19), channel_id=1, source_target_pairs={{1,0},{2,1},{3,2},{4,3},{5,4},{6,5},{7,6},{8,7},{9,8},{10,9},{11,1... | collective-permute-start | bytes 49160 | tf_op jit(solution)/shard_map/ppermute | solution.py:660
  40.0 11.9 %collective-permute-start.4 = (f32[64,128]{1,0:T(8,128)}, f32[64,128]{1,0:T(8,128)S(1)}, u32[]{:S(2)}, u32[]{:S(2)}) collective-permute-start(f32[64,128]{1,0:T(8,128)} %get-tuple-element.19), channel_id=1, source_target_pairs={{112,0},{0,16},{16,32},{32,48},{48,64},{64,80},{80,96},{96,112},{1... | collective-permute-start | bytes 98312 | tf_op jit(solution)/shard_map/ppermute | solution.py:660
  42.4 9.5 %collective-permute-start.5 = (f32[64,128]{1,0:T(8,128)}, f32[64,128]{1,0:T(8,128)S(1)}, u32[]{:S(2)}, u32[]{:S(2)}) collective-permute-start(f32[64,128]{1,0:T(8,128)} %get-tuple-element.19), channel_id=1, source_target_pairs={{16,0},{32,16},{48,32},{64,48},{80,64},{96,80},{112,96},{0,112},{1... | collective-permute-start | bytes 98312 | tf_op jit(solution)/shard_map/ppermute | solution.py:660
  51.9 13.0 %collective-permute-start.6 = (f32[3,64,128]{2,1,0:T(8,128)S(1)}, f32[3,64,128]{2,1,0:T(8,128)S(1)}, u32[]{:S(2)}, u32[]{:S(2)}) collective-permute-start(f32[3,64,128]{2,1,0:T(8,128)S(1)} %pad_maximum_fusion.9), channel_id=1, source_target_pairs={{15,0},{0,1},{1,2},{2,3},{3,4},{4,5},{5,6},{6,7},{7,8},{8,9},{9,10... | collective-permute-start | bytes 294920 | tf_op jit(solution)/shard_map/ppermute | solution.py:660
  52.0 12.9 %collective-permute-start.7 = (f32[3,64,128]{2,1,0:T(8,128)S(1)}, f32[3,64,128]{2,1,0:T(8,128)S(1)}, u32[]{:S(2)}, u32[]{:S(2)}) collective-permute-start(f32[3,64,128]{2,1,0:T(8,128)S(1)} %pad_maximum_fusion.9), channel_id=1, source_target_pairs={{1,0},{2,1},{3,2},{4,3},{5,4},{6,5},{7,6},{8,7},{9,8},{10,9},{11,1... | collective-permute-start | bytes 294920 | tf_op jit(solution)/shard_map/ppermute | solution.py:660
  184.2 10.5 %collective-permute-start.8 = (f32[3,48,128]{2,1,0:T(8,128)S(1)}, f32[3,48,128]{2,1,0:T(8,128)S(1)}, u32[]{:S(2)}, u32[]{:S(2)}) collective-permute-start(f32[3,48,128]{2,1,0:T(8,128)S(1)} %get-tuple-element.55), channel_id=1, source_target_pairs={{1,0},{2,1},{3,2},{4,3},{5,4},{6,5},{7,6},{8,7},{9,8},{10,9},{11,1... | collective-permute-start | bytes 221192 | tf_op jit(solution)/shard_map/ppermute | solution.py:660
  184.6 10.2 %collective-permute-start.9 = (f32[3,48,128]{2,1,0:T(8,128)S(1)}, f32[3,48,128]{2,1,0:T(8,128)S(1)}, u32[]{:S(2)}, u32[]{:S(2)}) collective-permute-start(f32[3,48,128]{2,1,0:T(8,128)S(1)} %get-tuple-element.54), channel_id=1, source_target_pairs={{15,0},{0,1},{1,2},{2,3},{3,4},{4,5},{5,6},{6,7},{7,8},{8,9},{9,10... | collective-permute-start | bytes 221192 | tf_op jit(solution)/shard_map/ppermute | solution.py:660
  196.1 17.5 %collective-permute-start.10 = (f32[48,128]{1,0:T(8,128)S(1)}, f32[48,128]{1,0:T(8,128)S(1)}, u32[]{:S(2)}, u32[]{:S(2)}) collective-permute-start(f32[48,128]{1,0:T(8,128)S(1)} %get-tuple-element.47), channel_id=1, source_target_pairs={{16,0},{32,16},{48,32},{64,48},{80,64},{96,80},{112,96},{0,112},{1... | collective-permute-start | bytes 73736 | tf_op jit(solution)/shard_map/ppermute | solution.py:660
  198.2 15.5 %collective-permute-start.11 = (f32[48,128]{1,0:T(8,128)S(1)}, f32[48,128]{1,0:T(8,128)S(1)}, u32[]{:S(2)}, u32[]{:S(2)}) collective-permute-start(f32[48,128]{1,0:T(8,128)S(1)} %get-tuple-element.46), channel_id=1, source_target_pairs={{112,0},{0,16},{16,32},{32,48},{48,64},{64,80},{80,96},{96,112},{1... | collective-permute-start | bytes 73736 | tf_op jit(solution)/shard_map/ppermute | solution.py:660
  224.3 5.8 %collective-permute-start.12 = (f32[8,384]{1,0:T(8,128)S(1)}, f32[8,384]{1,0:T(8,128)S(1)}, u32[]{:S(2)}, u32[]{:S(2)}) collective-permute-start(f32[8,384]{1,0:T(8,128)S(1)} %get-tuple-element.77), channel_id=1, source_target_pairs={{1,0},{2,1},{3,2},{4,3},{5,4},{6,5},{7,6},{8,7},{9,8},{10,9},{11,1... | collective-permute-start | bytes 36872 | tf_op jit(solution)/shard_map/ppermute | solution.py:660
  228.7 6.7 %collective-permute-start.13 = (f32[8,384]{1,0:T(8,128)S(1)}, f32[8,384]{1,0:T(8,128)S(1)}, u32[]{:S(2)}, u32[]{:S(2)}) collective-permute-start(f32[8,384]{1,0:T(8,128)S(1)} %get-tuple-element.76), channel_id=1, source_target_pairs={{15,0},{0,1},{1,2},{2,3},{3,4},{4,5},{5,6},{6,7},{7,8},{8,9},{9,10... | collective-permute-start | bytes 36872 | tf_op jit(solution)/shard_map/ppermute | solution.py:660
  230.1 11.8 %copy-start.7 = (f32[8,384]{1,0:T(8,128)}, f32[8,384]{1,0:T(8,128)S(1)}, u32[]{:S(2)}) copy-start(f32[8,384]{1,0:T(8,128)S(1)} %collective-permute-done.12.r1) | copy-start | bytes 36868
  236.1 5.7 %collective-permute-start.14 = (f32[8,128]{1,0:T(8,128)S(1)}, f32[8,128]{1,0:T(8,128)S(1)}, u32[]{:S(2)}, u32[]{:S(2)}) collective-permute-start(f32[8,128]{1,0:T(8,128)S(1)} %get-tuple-element.61), channel_id=1, source_target_pairs={{16,0},{32,16},{48,32},{64,48},{80,64},{96,80},{112,96},{0,112},{1... | collective-permute-start | bytes 12296 | tf_op jit(solution)/shard_map/ppermute | solution.py:660
  236.1 5.7 %collective-permute-start.15 = (f32[8,128]{1,0:T(8,128)S(1)}, f32[8,128]{1,0:T(8,128)S(1)}, u32[]{:S(2)}, u32[]{:S(2)}) collective-permute-start(f32[8,128]{1,0:T(8,128)S(1)} %get-tuple-element.60), channel_id=1, source_target_pairs={{112,0},{0,16},{16,32},{32,48},{48,64},{64,80},{80,96},{96,112},{1... | collective-permute-start | bytes 12296 | tf_op jit(solution)/shard_map/ppermute | solution.py:660
  (17 other events, 86.2 us)
